TPU v7x, 32 devices: a whole 2x2x4 slice. The times are simulated.
32 devices in a mesh: blk: 8 (over y, x, core), grp: 4 (over z).
Axes of the slice: x: 2, y: 2, z: 4, core: 2. Of those that a mesh axis runs over, the one named last changes fastest.
Arguments:
- picture_embedding_array: bfloat16 [8192, 1152], P(('blk', 'grp')), may hold values from -0.1875 to 0.1875
- caption_embedding_array: bfloat16 [8192, 1152], P(('blk', 'grp')), may hold values from -0.1875 to 0.1875
- sharpness_multiplier: float32 [1], replicated, may hold values from 8 to 16
- score_offset: float32 [1], replicated, may hold values from -6 to -3
Outputs:
- row_loss: float32 [8192], P(('blk', 'grp'))
- grad_images: float32 [8192, 1152], P(('blk', 'grp'))
- grad_texts: float32 [8192, 1152], P(('blk', 'grp'))
All inputs are finite; a program needn't handle non-finite values.
Results may differ from a plain program's by a relative error of at most 0.02.
Values may be sent and summed in bfloat16 or wider, within the bound.
A program may use at most 64 MiB of HBM per device.

v0:
```python
import functools

import jax
import jax.numpy as jnp
from jax import lax
from jax.experimental import pallas as pl
from jax.experimental.pallas import tpu as pltpu
from jax.sharding import PartitionSpec as P

KSTEPS = 8


def passed_along(block, axis, distance):
    devices = range(lax.axis_size(axis))
    route = [((i - distance) % len(devices), i) for i in devices]
    return lax.ppermute(block, axis, route)


def normalize(raw):
    computed_quantities = raw.astype(jnp.float32)
    inverse = lax.rsqrt(
        jnp.sum(computed_quantities * computed_quantities, axis=-1, keepdims=True) + 1e-06
    )
    return (computed_quantities * inverse, inverse)


def back_norm(unit32, inverse, grad_unit):
    along = jnp.sum(unit32 * grad_unit, axis=-1, keepdims=True)
    return inverse * (grad_unit - unit32 * along)


def pairwise_loss_terms(
    image_block_rows, text_block_rows, target_labels, smoothing_coefficient, block_displacement
):
    pair_logit_matrix = (
        smoothing_coefficient
        * lax.dot_general(
            image_block_rows,
            text_block_rows,
            (((1,), (1,)), ((), ())),
            preferred_element_type=jnp.float32,
        )
        + block_displacement
    )
    row_portion = jnp.sum(jax.nn.softplus(-target_labels * pair_logit_matrix), axis=-1)
    sigmoid_weights = (
        -target_labels * jax.nn.sigmoid(-target_labels * pair_logit_matrix) * smoothing_coefficient
    ).astype(jnp.bfloat16)
    return (row_portion, sigmoid_weights)


def image_side(sigmoid_weights, text_block_rows):
    return jnp.dot(sigmoid_weights, text_block_rows, preferred_element_type=jnp.float32)


def text_side(sigmoid_weights, image_block_rows):
    return lax.dot_general(
        sigmoid_weights,
        image_block_rows,
        (((0,), (0,)), ((), ())),
        preferred_element_type=jnp.float32,
    )


def on_device(picture_embedding_array, caption_embedding_array, sharpness_multiplier, score_offset):
    smoothing_coefficient = sharpness_multiplier[0]
    block_displacement = score_offset[0]
    rows = picture_embedding_array.shape[0]
    img_unit32, img_inverse = normalize(picture_embedding_array)
    txt_unit32, txt_inverse = normalize(caption_embedding_array)
    image_unit_vectors = img_unit32.astype(jnp.bfloat16)
    text_unit_vectors = txt_unit32.astype(jnp.bfloat16)
    positions = lax.broadcasted_iota(jnp.int32, (rows, rows), 0)
    columns = lax.broadcasted_iota(jnp.int32, (rows, rows), 1)
    initial_label_values = jnp.where(positions == columns, 1.0, -1.0).astype(jnp.float32)
    negative_labels = jnp.full((rows, rows), -1.0, jnp.float32)
    row_total_sum, sigmoid_weights = pairwise_loss_terms(
        image_unit_vectors,
        text_unit_vectors,
        initial_label_values,
        smoothing_coefficient,
        block_displacement,
    )
    grad_img = image_side(sigmoid_weights, text_unit_vectors)
    own_text = text_side(sigmoid_weights, image_unit_vectors)
    incoming_caption_groups = text_unit_vectors
    carried = own_text
    for hop_index in range(1, KSTEPS):
        incoming_caption_groups, carried = (
            passed_along(incoming_caption_groups, ("blk", "grp"), 1),
            passed_along(carried.astype(jnp.bfloat16), ("blk", "grp"), 1).astype(carried.dtype),
        )
        row_portion, sigmoid_weights = pairwise_loss_terms(
            image_unit_vectors,
            incoming_caption_groups,
            negative_labels,
            smoothing_coefficient,
            block_displacement,
        )
        row_total_sum = row_total_sum + row_portion
        grad_img = grad_img + image_side(sigmoid_weights, incoming_caption_groups)
        carried = carried + text_side(sigmoid_weights, image_unit_vectors)
    grad_txt = passed_along(carried.astype(jnp.bfloat16), ("blk", "grp"), 1 - KSTEPS).astype(
        carried.dtype
    )
    grad_images = back_norm(img_unit32, img_inverse, grad_img)
    grad_texts = back_norm(txt_unit32, txt_inverse, grad_txt)
    return (row_total_sum, grad_images, grad_texts)


MESH = pl.DeviceIdType.MESH
A_NEAR, B_NEAR, X_NEAR, A_FAR, B_FAR, F_FAR = range(6)
KINDS = 6
A_UP, A_DOWN, B_UP, B_DOWN, A_CORE, A_COLUMN, B_COLUMN, F_CORE, A_RELAY, B_RELAY = range(10)
SENDS = 10
LANES = 128
PARTS = 2


def column_kernel(
    columns,
    deep,
    scale_ref,
    offset_ref,
    img_ref,
    txt_ref,
    loss_ref,
    grad_img_ref,
    grad_txt_ref,
    held,
    total,
    losses,
    sums,
    loss_in,
    send_sem,
    recv_sem,
    sum_sem,
):
    blk = lax.axis_index("blk")
    z = lax.axis_index("grp")
    core = lax.rem(blk, 2)
    column = blk // 2
    onward = 1 - 2 * core
    after = lax.rem(column + onward + columns, columns)
    before = lax.rem(column - onward + columns, columns)
    sibling = (2 * column + 1 - core, z)
    above, below = (blk, z + 1), (blk, z - 1)
    after_same = (2 * after + core, z)
    before_same = (2 * before + core, z)
    before_other = (2 * before + 1 - core, z)
    rows, width = img_ref.shape
    scale, offset = scale_ref[0], offset_ref[0]

    def beyond(zp):
        return (zp - z) * onward > 0

    def short(zp):
        return (zp - z) * onward < 0

    def slot(kind, zp):
        return kind * deep + zp

    at_end = (z == 0) | (z == deep - 1)
    a_end = jnp.where(onward > 0, z == deep - 1, z == 0)
    b_end = jnp.where(onward > 0, z == 0, z == deep - 1)
    q_helper = jnp.where(onward > 0, z == deep - 2, z == 1)
    p_helper = jnp.where(onward > 0, z == 1, z == deep - 2)
    helper = (z == 1) | (z == deep - 2)
    end = jnp.where(z == 1, 0, deep - 1)
    last = deep - 1 - end
    inner = (blk, jnp.where(z == 0, 1, deep - 2))
    outer = (blk, end)

    def has_a(zp):
        return (zp == z) | jnp.logical_not(b_end)

    def has_b(zp):
        return (zp == z) | jnp.logical_not(a_end)

    def a_goes_up(zp):
        return has_a(zp) & (zp <= z) & ((z < deep - 2) | ((z == deep - 2) & (onward > 0)))

    def a_goes_down(zp):
        return has_a(zp) & (zp >= z) & ((z > 1) | ((z == 1) & (onward < 0)))

    def b_goes_up(zp):
        return has_b(zp) & (zp <= z) & ((z < deep - 2) | ((z == deep - 2) & (onward < 0)))

    def b_goes_down(zp):
        return has_b(zp) & (zp >= z) & ((z > 1) | ((z == 1) & (onward > 0)))

    def crosses(zp):
        return (beyond(zp) & jnp.logical_not(b_end)) | ((zp == z) & p_helper)

    def a_to_column(zp):
        relayed = q_helper & (zp == end)
        return (crosses(zp) & jnp.logical_not(relayed)) | ((zp == z) & a_end)

    def b_to_column(zp):
        return has_b(zp) & jnp.logical_not(helper & (zp == end))

    def has_b_far(zp):
        return (zp == z) | jnp.logical_not(b_end)

    def has_f(zp):
        return (short(zp) & jnp.logical_not(a_end)) | ((zp == z) & q_helper)

    def has_x(zp):
        return (zp == z) | jnp.logical_not(a_end)

    size = rows // PARTS

    def transfer(send, source, target, zp, device, part):
        here = pl.ds(part * size, size)
        return pltpu.make_async_remote_copy(
            src_ref=held.at[slot(source, zp), here],
            dst_ref=held.at[slot(target, zp), here],
            send_sem=send_sem.at[send * deep + zp, part],
            recv_sem=recv_sem.at[slot(target, zp), part],
            device_id=device,
            device_id_type=MESH,
        )

    def arrived(kind, zp, part):
        transfer(A_UP, kind, kind, zp, sibling, part).wait_recv()

    def sent(send, zp):
        for part in range(PARTS):
            transfer(send, A_NEAR, A_NEAR, zp, sibling, part).wait_send()

    def unit(ref):
        raw = ref[...].astype(jnp.float32)
        inverse = lax.rsqrt(jnp.sum(raw * raw, axis=-1, keepdims=True) + 1e-06)
        return raw * inverse, inverse

    @pl.when(core == 0)
    def _():
        held[slot(A_NEAR, z)] = unit(txt_ref)[0].astype(jnp.bfloat16)
        held[slot(B_NEAR, z)] = unit(img_ref)[0].astype(jnp.bfloat16)

    @pl.when(core == 1)
    def _():
        held[slot(A_NEAR, z)] = unit(img_ref)[0].astype(jnp.bfloat16)
        held[slot(B_NEAR, z)] = unit(txt_ref)[0].astype(jnp.bfloat16)

    barrier = pltpu.get_barrier_semaphore()
    for device in (sibling, after_same, before_same, before_other):
        pl.semaphore_signal(barrier, inc=1, device_id=device, device_id_type=MESH)

    @pl.when(z < deep - 1)
    def _():
        pl.semaphore_signal(barrier, inc=1, device_id=above, device_id_type=MESH)

    @pl.when(z > 0)
    def _():
        pl.semaphore_signal(barrier, inc=1, device_id=below, device_id_type=MESH)

    total[...] = jnp.zeros_like(total)
    losses[...] = jnp.zeros_like(losses)
    edges = jnp.where(z > 0, 1, 0) + jnp.where(z < deep - 1, 1, 0)
    pl.semaphore_wait(barrier, 4 + edges)

    def pass_b(zp, distance, part):
        @pl.when(has_b(zp) & (distance > 0))
        def _():
            arrived(B_NEAR, zp, part)

        @pl.when(b_goes_up(zp))
        def _():
            transfer(B_UP, B_NEAR, B_NEAR, zp, above, part).start()

        @pl.when(b_goes_down(zp))
        def _():
            transfer(B_DOWN, B_NEAR, B_NEAR, zp, below, part).start()

        @pl.when(b_to_column(zp))
        def _():
            transfer(B_COLUMN, B_NEAR, B_FAR, zp, before_other, part).start()

    def pass_a(zp, distance, part):
        @pl.when(has_a(zp) & (distance > 0))
        def _():
            arrived(A_NEAR, zp, part)

        @pl.when(a_goes_up(zp))
        def _():
            transfer(A_UP, A_NEAR, A_NEAR, zp, above, part).start()

        @pl.when(a_goes_down(zp))
        def _():
            transfer(A_DOWN, A_NEAR, A_NEAR, zp, below, part).start()

        @pl.when(a_to_column(zp))
        def _():
            transfer(A_COLUMN, A_NEAR, A_FAR, zp, after_same, part).start()

        @pl.when(has_a(zp))
        def _():
            transfer(A_CORE, A_NEAR, X_NEAR, zp, sibling, part).start()

    def relay():
        for part in range(PARTS):
            arrived(B_FAR, z, part)
            transfer(B_RELAY, B_FAR, B_FAR, z, inner, part).start()

            @pl.when(a_end)
            def _():
                arrived(A_FAR, z, part)
                transfer(A_RELAY, A_FAR, A_FAR, z, inner, part).start()

    def sum_copy():
        return pltpu.make_async_remote_copy(
            src_ref=sums.at[0],
            dst_ref=sums.at[1],
            send_sem=sum_sem.at[0],
            recv_sem=sum_sem.at[1],
            device_id=outer,
            device_id_type=MESH,
        )

    def loss_copy():
        return pltpu.make_async_remote_copy(
            src_ref=losses.at[2],
            dst_ref=loss_in,
            send_sem=sum_sem.at[2],
            recv_sem=sum_sem.at[3],
            device_id=outer,
            device_id_type=MESH,
        )

    diagonal = lax.broadcasted_iota(jnp.int32, (rows, rows), 0) == lax.broadcasted_iota(
        jnp.int32, (rows, rows), 1
    )

    def meet(role, own, other, same):
        logits = (
            scale
            * lax.dot_general(
                held[own],
                held[other],
                (((1,), (1,)), ((), ())),
                preferred_element_type=jnp.float32,
            )
            + offset
        )
        sign = jnp.where(diagonal & same, -1.0, 1.0)
        turned = sign * logits
        small = jnp.exp(-jnp.abs(turned))
        loss = jnp.maximum(turned, 0.0) + jnp.log1p(small)
        sigmoid = jnp.where(turned >= 0.0, 1.0, small) / (1.0 + small)
        weights = (sign * sigmoid * scale).astype(jnp.bfloat16)
        part = loss[:, :LANES]
        for at in range(LANES, rows, LANES):
            part = part + loss[:, at : at + LANES]
        losses[role] += part
        step = 384 if width % 384 == 0 else width
        for at in range(0, width, step):
            total[role, :, at : at + step] += jnp.dot(
                weights, held[other, :, at : at + step], preferred_element_type=jnp.float32
            )

    own_a, own_b = slot(A_NEAR, z), slot(B_NEAR, z)

    def near(zp):
        first = jnp.where(short(zp), 0, jnp.where(beyond(zp), 1, 0))

        def tile(which, carry):
            @pl.when((which == 2) & has_x(zp))
            def _():
                for part in range(PARTS):
                    arrived(X_NEAR, zp, part)

            role = jnp.where(which == 0, 0, 1)
            kind = jnp.where(which == 0, A_NEAR, jnp.where(which == 1, B_NEAR, X_NEAR))
            own = jnp.where(which == 0, own_b, own_a)

            @pl.when(((which == 2) & has_x(zp)) | (which == first) | (zp == z))
            def _():
                meet(role, own, slot(kind, zp), (which < 2) & (zp == z))

            return carry

        lax.fori_loop(0, 3, tile, 0)

    def far(zp):
        @pl.when(has_b_far(zp))
        def _():
            for part in range(PARTS):

                @pl.when(jnp.logical_not(at_end & (zp == z)))
                def _():
                    arrived(B_FAR, zp, part)

                @pl.when(crosses(zp))
                def _():
                    transfer(F_CORE, B_FAR, F_FAR, zp, sibling, part).start()

        helps = helper & (zp != end)

        def tile(which, carry):
            for part in range(PARTS):

                @pl.when((which == 1) & crosses(zp))
                def _():
                    arrived(A_FAR, zp, part)

                @pl.when((which == 1) & has_f(zp))
                def _():
                    arrived(F_FAR, zp, part)

            helping = which < 2
            kind_0 = jnp.where(q_helper, X_NEAR, B_FAR)
            kind_1 = jnp.where(q_helper, F_FAR, A_FAR)
            kind_3 = jnp.where(short(zp), F_FAR, A_FAR)
            kind = jnp.where(
                which == 0,
                kind_0,
                jnp.where(which == 1, kind_1, jnp.where(which == 2, B_FAR, kind_3)),
            )
            in_q = (which == 3) & short(zp)
            own_end = jnp.where(q_helper, slot(A_NEAR, end), slot(B_NEAR, end))
            own = jnp.where(helping, own_end, jnp.where(in_q, own_a, own_b))
            role = jnp.where(helping, 2, jnp.where(in_q, 1, 0))
            other = (zp != z) & jnp.logical_not(at_end)

            @pl.when(
                (helping & helps)
                | ((which == 2) & has_b_far(zp))
                | ((which == 3) & other)
            )
            def _():
                meet(role, own, slot(kind, zp), False)

            @pl.when((which == 1) & helper & (zp == last))
            def _():
                sums[0] = total[2].astype(jnp.bfloat16)
                sum_copy().start()
                loss_copy().start()

            return carry

        lax.fori_loop(0, 4, tile, 0)

    def both_ways(distance, action):
        @pl.when((distance >= 0) & (distance < deep) & (z - distance >= 0))
        def _():
            action(z - distance)

        @pl.when((distance > 0) & (z + distance < deep))
        def _():
            action(z + distance)

    def turn(distance, carry):
        for step in (pass_b, pass_a):
            for part in range(PARTS):
                both_ways(distance, functools.partial(step, distance=distance, part=part))
        both_ways(distance, near)
        pl.when((distance == 0) & at_end)(relay)
        both_ways(distance - 1, far)
        return carry

    lax.fori_loop(0, deep + 1, turn, 0)

    @pl.when(at_end)
    def _():
        sum_copy().wait_recv()
        loss_copy().wait_recv()
        role = jnp.where(a_end, 1, 0)
        total[role] += sums[1].astype(jnp.float32)
        losses[role] += loss_in[...]

    def finish(ref, role):
        unit32, inverse = unit(ref)
        grad = total[role]
        along = jnp.sum(unit32 * grad, axis=-1, keepdims=True)
        return inverse * (grad - unit32 * along)

    grad_img_ref[...] = finish(img_ref, core)
    grad_txt_ref[...] = finish(txt_ref, 1 - core)
    loss_ref[...] = jnp.sum(losses[core], axis=-1, keepdims=True)

    def settle(zp, carry):
        for went, send in (
            (a_goes_up(zp), A_UP),
            (a_goes_down(zp), A_DOWN),
            (b_goes_up(zp), B_UP),
            (b_goes_down(zp), B_DOWN),
            (has_a(zp), A_CORE),
            (a_to_column(zp), A_COLUMN),
            (b_to_column(zp), B_COLUMN),
            (crosses(zp), F_CORE),
            ((zp == z) & a_end, A_RELAY),
            ((zp == z) & at_end, B_RELAY),
        ):
            pl.when(went)(functools.partial(sent, send, zp))
        return carry

    lax.fori_loop(0, deep, settle, 0)

    @pl.when(helper)
    def _():
        sum_copy().wait_send()
        loss_copy().wait_send()


def on_column(columns, deep, images, texts, scale, offset):
    rows, width = images.shape
    tiles = 4 * deep
    loss, grad_images, grad_texts = pl.pallas_call(
        functools.partial(column_kernel, columns, deep),
        out_shape=(
            jax.ShapeDtypeStruct((rows, 1), jnp.float32),
            jax.ShapeDtypeStruct((rows, width), jnp.float32),
            jax.ShapeDtypeStruct((rows, width), jnp.float32),
        ),
        in_specs=[pl.BlockSpec(memory_space=pltpu.SMEM)] * 2
        + [pl.BlockSpec(memory_space=pltpu.VMEM)] * 2,
        out_specs=[pl.BlockSpec(memory_space=pltpu.VMEM)] * 3,
        scratch_shapes=[
            pltpu.VMEM((KINDS * deep, rows, width), jnp.bfloat16),
            pltpu.VMEM((3, rows, width), jnp.float32),
            pltpu.VMEM((3, rows, LANES), jnp.float32),
            pltpu.VMEM((2, rows, width), jnp.bfloat16),
            pltpu.VMEM((rows, LANES), jnp.float32),
            pltpu.SemaphoreType.DMA((SENDS * deep, PARTS)),
            pltpu.SemaphoreType.DMA((KINDS * deep, PARTS)),
            pltpu.SemaphoreType.DMA((4,)),
        ],
        compiler_params=pltpu.CompilerParams(
            collective_id=0, has_side_effects=True, vmem_limit_bytes=48 * 1024 * 1024
        ),
        cost_estimate=pl.CostEstimate(
            flops=tiles * 4 * rows * rows * width,
            bytes_accessed=12 * rows * width,
            transcendentals=tiles * 3 * rows * rows,
        ),
        name="column",
    )(scale, offset, images, texts)
    return loss.reshape(rows), grad_images, grad_texts


def solution(mesh):
    blocks, deep = mesh.shape["blk"], mesh.shape["grp"]
    body = on_device
    if KSTEPS == 2 * deep and deep >= 4 and blocks % 2 == 0 and blocks >= 6:
        body = functools.partial(on_column, blocks // 2, deep)
    return jax.shard_map(
        body,
        mesh=mesh,
        in_specs=(P(("blk", "grp"), None), P(("blk", "grp"), None), P(), P()),
        out_specs=(P(("blk", "grp")), P(("blk", "grp"), None), P(("blk", "grp"), None)),
        check_vma=False,
    )
```

profile of v0, /device:TPU:1, one launch (start us, length us, event | category | flops | bytes accessed | tf_op | source)
XLA Modules:
  0.0 97.9 jit_solution(9514671422284480240)
XLA Ops:
  1.9 0.0 copy-start
  1.9 1.1 %copy-done = bf16[256,1152]{1,0:T(8,128)(2,1)S(1)} copy-done((bf16[256,1152]{1,0:T(8,128)(2,1)S(1)}, bf16[256,1152]{1,0:T(8,128)(2,1)}, u32[]{:S(2)}) %copy-start) | copy-done | bytes 589848
  3.0 0.0 copy-start.1
  3.0 1.1 %copy-done.1 = bf16[256,1152]{1,0:T(8,128)(2,1)S(1)} copy-done((bf16[256,1152]{1,0:T(8,128)(2,1)S(1)}, bf16[256,1152]{1,0:T(8,128)(2,1)}, u32[]{:S(2)}) %copy-start.1) | copy-done | bytes 589848
  4.1 91.1 %column.1 = (f32[256,1]{1,0:T(8,128)S(1)}, f32[256,1152]{1,0:T(8,128)S(1)}, f32[256,1152]{1,0:T(8,128)S(1)}) custom-call(f32[1]{0:T(128)S(6)} %copy.9.scale_ref, f32[1]{0:T(128)S(6)} %copy.10.offset_ref, bf16[256,1152]{1,0:T(8,128)(2,1)S(1)} %copy-done, bf16[256,1152]{1,0:T(8,128)(2,1)S(1)} %copy-done.1), custom_call_target="tpu_custom_call" | custom-call | flops 4831838208 | bytes 3538944 | tf_op jit(solution)/shard_map/column/pallas_call | solution.py:509
  95.2 0.7 reduce
  95.9 1.0 %copy.11 = f32[256,1152]{1,0:T(8,128)} copy(f32[256,1152]{1,0:T(8,128)S(1)} %get-tuple-element.13) | data formatting | bytes 2359296
  96.9 1.0 %copy.12 = f32[256,1152]{1,0:T(8,128)} copy(f32[256,1152]{1,0:T(8,128)S(1)} %get-tuple-element.14) | data formatting | bytes 2359296
Async XLA Ops:
  1.9 1.1 %copy-start = (bf16[256,1152]{1,0:T(8,128)(2,1)S(1)}, bf16[256,1152]{1,0:T(8,128)(2,1)}, u32[]{:S(2)}) copy-start(bf16[256,1152]{1,0:T(8,128)(2,1)} %img_ref.1) | copy-start | bytes 1769476
  3.0 1.1 %copy-start.1 = (bf16[256,1152]{1,0:T(8,128)(2,1)S(1)}, bf16[256,1152]{1,0:T(8,128)(2,1)}, u32[]{:S(2)}) copy-start(bf16[256,1152]{1,0:T(8,128)(2,1)} %txt_ref.1) | copy-start | bytes 1769476
where the time goes:
time: 98.5 us; the launch traced here: 97.9 us
  Pallas kernels  91.1 us (92%)
  local copies, waits for them, and re-layouts  4.15 us (4%)
  between operations  1.94 us (2%)
    pallas_call x1, Pallas kernels, on_column(): pl.pallas_call(functools.partial(column_kernel, columns, deep), out_shape...  91.1 us
    unnamed x6, local copies, waits for them, and re-layouts  4.15 us

commit v1 on v0

--- a/solution.py
+++ b/solution.py
@@ -114,6 +114,7 @@
 A_UP, A_DOWN, B_UP, B_DOWN, A_CORE, A_COLUMN, B_COLUMN, F_CORE, A_RELAY, B_RELAY = range(10)
 SENDS = 10
 LANES = 128
+LOG2E = 1.4426950408889634
 PARTS = 2
 
 
@@ -332,32 +333,50 @@
         jnp.int32, (rows, rows), 1
     )
 
-    def meet(role, own, other, same):
-        logits = (
-            scale
-            * lax.dot_general(
-                held[own],
-                held[other],
-                (((1,), (1,)), ((), ())),
-                preferred_element_type=jnp.float32,
-            )
-            + offset
-        )
-        sign = jnp.where(diagonal & same, -1.0, 1.0)
-        turned = sign * logits
+    def weigh(role, own, other, pairs, with_loss):
+        dots = lax.dot_general(
+            held[own],
+            held[other],
+            (((1,), (1,)), ((), ())),
+            preferred_element_type=jnp.float32,
+        )
+        if not with_loss:
+            power = jnp.exp2(dots * (-LOG2E * scale) - LOG2E * offset)
+            return (scale / (1.0 + power)).astype(jnp.bfloat16)
+        logits = scale * dots + offset
+        turned = jnp.where(diagonal, -logits, logits) if pairs else logits
         small = jnp.exp(-jnp.abs(turned))
         loss = jnp.maximum(turned, 0.0) + jnp.log1p(small)
-        sigmoid = jnp.where(turned >= 0.0, 1.0, small) / (1.0 + small)
-        weights = (sign * sigmoid * scale).astype(jnp.bfloat16)
         part = loss[:, :LANES]
         for at in range(LANES, rows, LANES):
             part = part + loss[:, at : at + LANES]
         losses[role] += part
-        step = 384 if width % 384 == 0 else width
-        for at in range(0, width, step):
-            total[role, :, at : at + step] += jnp.dot(
-                weights, held[other, :, at : at + step], preferred_element_type=jnp.float32
-            )
+        weights = jnp.where(turned >= 0.0, scale, scale * small) / (1.0 + small)
+        if pairs:
+            weights = jnp.where(diagonal, -weights, weights)
+        return weights.astype(jnp.bfloat16)
+
+    def meet(role, own, other, pairs):
+        def add(with_loss):
+            weights = weigh(role, own, other, pairs, with_loss)
+            step = 384 if width % 384 == 0 else width
+            for at in range(0, width, step):
+                total[role, :, at : at + step] += jnp.dot(
+                    weights, held[other, :, at : at + step], preferred_element_type=jnp.float32
+                )
+
+        if pairs:
+            add(True)
+            return
+        of_image = (role == core) | ((role == 2) & (z == 1))
+
+        @pl.when(of_image)
+        def _():
+            add(True)
+
+        @pl.when(jnp.logical_not(of_image))
+        def _():
+            add(False)
 
     own_a, own_b = slot(A_NEAR, z), slot(B_NEAR, z)
 
@@ -374,9 +393,13 @@
             kind = jnp.where(which == 0, A_NEAR, jnp.where(which == 1, B_NEAR, X_NEAR))
             own = jnp.where(which == 0, own_b, own_a)
 
-            @pl.when(((which == 2) & has_x(zp)) | (which == first) | (zp == z))
+            @pl.when((which < 2) & (zp == z))
             def _():
-                meet(role, own, slot(kind, zp), (which < 2) & (zp == z))
+                meet(role, own, slot(kind, zp), True)
+
+            @pl.when(((which == 2) & has_x(zp)) | ((which == first) & (zp != z)))
+            def _():
+                meet(role, own, slot(kind, zp), False)
 
             return carry
 

time: 98.5 us -> 98.4 us (level)
  no operation moved by 1% of the time
where the time goes in v1:
time: 98.4 us; the launch traced here: 97.8 us
  Pallas kernels  91.1 us (93%)
  local copies, waits for them, and re-layouts  4.15 us (4%)
  between operations  1.94 us (2%)
    pallas_call x1, Pallas kernels, on_column(): pl.pallas_call(functools.partial(column_kernel, columns, deep), out_shape...  91.1 us
    unnamed x6, local copies, waits for them, and re-layouts  4.15 us

profile of v1, /device:TPU:1, one launch (start us, length us, event | category | flops | bytes accessed | tf_op | source)
XLA Modules:
  0.0 97.8 jit_solution(168362909091771679)
XLA Ops:
  1.9 0.0 copy-start
  1.9 1.1 %copy-done = bf16[256,1152]{1,0:T(8,128)(2,1)S(1)} copy-done((bf16[256,1152]{1,0:T(8,128)(2,1)S(1)}, bf16[256,1152]{1,0:T(8,128)(2,1)}, u32[]{:S(2)}) %copy-start) | copy-done | bytes 589848
  3.0 0.0 copy-start.1
  3.0 1.1 %copy-done.1 = bf16[256,1152]{1,0:T(8,128)(2,1)S(1)} copy-done((bf16[256,1152]{1,0:T(8,128)(2,1)S(1)}, bf16[256,1152]{1,0:T(8,128)(2,1)}, u32[]{:S(2)}) %copy-start.1) | copy-done | bytes 589848
  4.1 91.1 %column.1 = (f32[256,1]{1,0:T(8,128)S(1)}, f32[256,1152]{1,0:T(8,128)S(1)}, f32[256,1152]{1,0:T(8,128)S(1)}) custom-call(f32[1]{0:T(128)S(6)} %copy.9.scale_ref, f32[1]{0:T(128)S(6)} %copy.10.offset_ref, bf16[256,1152]{1,0:T(8,128)(2,1)S(1)} %copy-done, bf16[256,1152]{1,0:T(8,128)(2,1)S(1)} %copy-done.1), custom_call_target="tpu_custom_call" | custom-call | flops 4831838208 | bytes 3538944 | tf_op jit(solution)/shard_map/column/pallas_call | solution.py:532
  95.1 0.7 reduce
  95.8 1.0 %copy.11 = f32[256,1152]{1,0:T(8,128)} copy(f32[256,1152]{1,0:T(8,128)S(1)} %get-tuple-element.13) | data formatting | bytes 2359296
  96.8 1.0 %copy.12 = f32[256,1152]{1,0:T(8,128)} copy(f32[256,1152]{1,0:T(8,128)S(1)} %get-tuple-element.14) | data formatting | bytes 2359296
Async XLA Ops:
  1.9 1.1 %copy-start = (bf16[256,1152]{1,0:T(8,128)(2,1)S(1)}, bf16[256,1152]{1,0:T(8,128)(2,1)}, u32[]{:S(2)}) copy-start(bf16[256,1152]{1,0:T(8,128)(2,1)} %img_ref.1) | copy-start | bytes 1769476
  3.0 1.1 %copy-start.1 = (bf16[256,1152]{1,0:T(8,128)(2,1)S(1)}, bf16[256,1152]{1,0:T(8,128)(2,1)}, u32[]{:S(2)}) copy-start(bf16[256,1152]{1,0:T(8,128)(2,1)} %txt_ref.1) | copy-start | bytes 1769476

commit v2 on v1

--- a/solution.py
+++ b/solution.py
@@ -172,26 +172,31 @@
     inner = (blk, jnp.where(z == 0, 1, deep - 2))
     outer = (blk, end)
 
+    final = jnp.where(end == 0, deep - 2, 1)
+
+    def through(zp):
+        return (zp == z) | (zp == deep - 1 - z)
+
     def has_a(zp):
-        return (zp == z) | jnp.logical_not(b_end)
+        return through(zp) | jnp.logical_not(b_end)
 
     def has_b(zp):
-        return (zp == z) | jnp.logical_not(a_end)
+        return through(zp) | jnp.logical_not(a_end)
 
     def a_goes_up(zp):
-        return has_a(zp) & (zp <= z) & ((z < deep - 2) | ((z == deep - 2) & (onward > 0)))
+        return has_a(zp) & (zp <= z) & ((z < deep - 2) | ((z == deep - 2) & ((onward > 0) | (zp == 0))))
 
     def a_goes_down(zp):
-        return has_a(zp) & (zp >= z) & ((z > 1) | ((z == 1) & (onward < 0)))
+        return has_a(zp) & (zp >= z) & ((z > 1) | ((z == 1) & ((onward < 0) | (zp == deep - 1))))
 
     def b_goes_up(zp):
-        return has_b(zp) & (zp <= z) & ((z < deep - 2) | ((z == deep - 2) & (onward < 0)))
+        return has_b(zp) & (zp <= z) & ((z < deep - 2) | ((z == deep - 2) & ((onward < 0) | (zp == 0))))
 
     def b_goes_down(zp):
-        return has_b(zp) & (zp >= z) & ((z > 1) | ((z == 1) & (onward > 0)))
+        return has_b(zp) & (zp >= z) & ((z > 1) | ((z == 1) & ((onward > 0) | (zp == deep - 1))))
 
     def crosses(zp):
-        return (beyond(zp) & jnp.logical_not(b_end)) | ((zp == z) & p_helper)
+        return (beyond(zp) & (through(zp) | jnp.logical_not(b_end))) | ((zp == z) & p_helper)
 
     def a_to_column(zp):
         relayed = q_helper & (zp == end)
@@ -201,13 +206,13 @@
         return has_b(zp) & jnp.logical_not(helper & (zp == end))
 
     def has_b_far(zp):
-        return (zp == z) | jnp.logical_not(b_end)
+        return through(zp) | jnp.logical_not(b_end)
 
     def has_f(zp):
-        return (short(zp) & jnp.logical_not(a_end)) | ((zp == z) & q_helper)
+        return (short(zp) & (through(zp) | jnp.logical_not(a_end))) | ((zp == z) & q_helper)
 
     def has_x(zp):
-        return (zp == z) | jnp.logical_not(a_end)
+        return through(zp) | jnp.logical_not(a_end)
 
     size = rows // PARTS
 
@@ -418,7 +423,7 @@
                 def _():
                     transfer(F_CORE, B_FAR, F_FAR, zp, sibling, part).start()
 
-        helps = helper & (zp != end)
+        helps = helper & (zp != end) & (zp != last)
 
         def tile(which, carry):
             for part in range(PARTS):
@@ -444,7 +449,7 @@
             own_end = jnp.where(q_helper, slot(A_NEAR, end), slot(B_NEAR, end))
             own = jnp.where(helping, own_end, jnp.where(in_q, own_a, own_b))
             role = jnp.where(helping, 2, jnp.where(in_q, 1, 0))
-            other = (zp != z) & jnp.logical_not(at_end)
+            other = (zp != z) & (through(zp) | jnp.logical_not(at_end))
 
             @pl.when(
                 (helping & helps)
@@ -454,24 +459,31 @@
             def _():
                 meet(role, own, slot(kind, zp), False)
 
-            @pl.when((which == 1) & helper & (zp == last))
+            @pl.when((which == 1) & helper & (zp == final))
             def _():
                 sums[0] = total[2].astype(jnp.bfloat16)
                 sum_copy().start()
-                loss_copy().start()
+
+                @pl.when(z == 1)
+                def _():
+                    loss_copy().start()
 
             return carry
 
         lax.fori_loop(0, 4, tile, 0)
 
+    inward = jnp.where(z < deep // 2, 1, -1)
+
     def both_ways(distance, action):
-        @pl.when((distance >= 0) & (distance < deep) & (z - distance >= 0))
-        def _():
-            action(z - distance)
-
-        @pl.when((distance > 0) & (z + distance < deep))
-        def _():
-            action(z + distance)
+        ahead, behind = z + inward * distance, z - inward * distance
+
+        @pl.when((distance >= 0) & (distance < deep) & (ahead >= 0) & (ahead < deep))
+        def _():
+            action(ahead)
+
+        @pl.when((distance > 0) & (behind >= 0) & (behind < deep))
+        def _():
+            action(behind)
 
     def turn(distance, carry):
         for step in (pass_b, pass_a):
@@ -487,10 +499,13 @@
     @pl.when(at_end)
     def _():
         sum_copy().wait_recv()
-        loss_copy().wait_recv()
         role = jnp.where(a_end, 1, 0)
         total[role] += sums[1].astype(jnp.float32)
-        losses[role] += loss_in[...]
+
+        @pl.when(z == 0)
+        def _():
+            loss_copy().wait_recv()
+            losses[role] += loss_in[...]
 
     def finish(ref, role):
         unit32, inverse = unit(ref)
@@ -523,7 +538,7 @@
     @pl.when(helper)
     def _():
         sum_copy().wait_send()
-        loss_copy().wait_send()
+        pl.when(z == 1)(lambda: loss_copy().wait_send())
 
 
 def on_column(columns, deep, images, texts, scale, offset):

time: 98.4 us -> 93.7 us (0.952)
  Pallas kernels: 91.1 us -> 86.4 us
    pallas_call x1, Pallas kernels: 91.1 us -> 86.4 us  [on_column(): pl.pallas_call(functools.partial(column_kernel, columns, deep), out_shape...]
where the time goes in v2:
time: 93.7 us; the launch traced here: 93.1 us
  Pallas kernels  86.4 us (92%)
  local copies, waits for them, and re-layouts  4.15 us (4%)
  between operations  1.94 us (2%)
    pallas_call x1, Pallas kernels, on_column(): pl.pallas_call(functools.partial(column_kernel, columns, deep), out_shape...  86.4 us
    unnamed x6, local copies, waits for them, and re-layouts  4.15 us

profile of v2, /device:TPU:1, one launch (start us, length us, event | category | flops | bytes accessed | tf_op | source)
XLA Modules:
  0.0 93.1 jit_solution(2734869956994727362)
XLA Ops:
  1.9 0.0 copy-start
  1.9 1.1 %copy-done = bf16[256,1152]{1,0:T(8,128)(2,1)S(1)} copy-done((bf16[256,1152]{1,0:T(8,128)(2,1)S(1)}, bf16[256,1152]{1,0:T(8,128)(2,1)}, u32[]{:S(2)}) %copy-start) | copy-done | bytes 589848
  3.0 0.0 copy-start.1
  3.0 1.1 %copy-done.1 = bf16[256,1152]{1,0:T(8,128)(2,1)S(1)} copy-done((bf16[256,1152]{1,0:T(8,128)(2,1)S(1)}, bf16[256,1152]{1,0:T(8,128)(2,1)}, u32[]{:S(2)}) %copy-start.1) | copy-done | bytes 589848
  4.1 86.4 %column.1 = (f32[256,1]{1,0:T(8,128)S(1)}, f32[256,1152]{1,0:T(8,128)S(1)}, f32[256,1152]{1,0:T(8,128)S(1)}) custom-call(f32[1]{0:T(128)S(6)} %copy.9.scale_ref, f32[1]{0:T(128)S(6)} %copy.10.offset_ref, bf16[256,1152]{1,0:T(8,128)(2,1)S(1)} %copy-done, bf16[256,1152]{1,0:T(8,128)(2,1)S(1)} %copy-done.1), custom_call_target="tpu_custom_call" | custom-call | flops 4831838208 | bytes 3538944 | tf_op jit(solution)/shard_map/column/pallas_call | solution.py:547
  90.4 0.7 reduce
  91.1 1.0 %copy.11 = f32[256,1152]{1,0:T(8,128)} copy(f32[256,1152]{1,0:T(8,128)S(1)} %get-tuple-element.13) | data formatting | bytes 2359296
  92.1 1.0 %copy.12 = f32[256,1152]{1,0:T(8,128)} copy(f32[256,1152]{1,0:T(8,128)S(1)} %get-tuple-element.14) | data formatting | bytes 2359296
Async XLA Ops:
  1.9 1.1 %copy-start = (bf16[256,1152]{1,0:T(8,128)(2,1)S(1)}, bf16[256,1152]{1,0:T(8,128)(2,1)}, u32[]{:S(2)}) copy-start(bf16[256,1152]{1,0:T(8,128)(2,1)} %img_ref.1) | copy-start | bytes 1769476
  3.0 1.1 %copy-start.1 = (bf16[256,1152]{1,0:T(8,128)(2,1)S(1)}, bf16[256,1152]{1,0:T(8,128)(2,1)}, u32[]{:S(2)}) copy-start(bf16[256,1152]{1,0:T(8,128)(2,1)} %txt_ref.1) | copy-start | bytes 1769476

commit v3 on v2

--- a/solution.py
+++ b/solution.py
@@ -123,8 +123,8 @@
     deep,
     scale_ref,
     offset_ref,
-    img_ref,
-    txt_ref,
+    img_hbm,
+    txt_hbm,
     loss_ref,
     grad_img_ref,
     grad_txt_ref,
@@ -132,7 +132,9 @@
     total,
     losses,
     sums,
-    loss_in,
+    loss_row,
+    raw,
+    raw_sem,
     send_sem,
     recv_sem,
     sum_sem,
@@ -149,7 +151,13 @@
     after_same = (2 * after + core, z)
     before_same = (2 * before + core, z)
     before_other = (2 * before + 1 - core, z)
-    rows, width = img_ref.shape
+    rows, width = img_hbm.shape
+    copies = [
+        pltpu.make_async_copy(source, raw.at[at], raw_sem.at[at])
+        for at, source in enumerate((img_hbm, txt_hbm))
+    ]
+    for copy in copies:
+        copy.start()
     scale, offset = scale_ref[0], offset_ref[0]
 
     def beyond(zp):
@@ -234,20 +242,10 @@
         for part in range(PARTS):
             transfer(send, A_NEAR, A_NEAR, zp, sibling, part).wait_send()
 
-    def unit(ref):
-        raw = ref[...].astype(jnp.float32)
-        inverse = lax.rsqrt(jnp.sum(raw * raw, axis=-1, keepdims=True) + 1e-06)
-        return raw * inverse, inverse
-
-    @pl.when(core == 0)
-    def _():
-        held[slot(A_NEAR, z)] = unit(txt_ref)[0].astype(jnp.bfloat16)
-        held[slot(B_NEAR, z)] = unit(img_ref)[0].astype(jnp.bfloat16)
-
-    @pl.when(core == 1)
-    def _():
-        held[slot(A_NEAR, z)] = unit(img_ref)[0].astype(jnp.bfloat16)
-        held[slot(B_NEAR, z)] = unit(txt_ref)[0].astype(jnp.bfloat16)
+    def unit(which):
+        values = raw[which].astype(jnp.float32)
+        inverse = lax.rsqrt(jnp.sum(values * values, axis=-1, keepdims=True) + 1e-06)
+        return values * inverse, inverse
 
     barrier = pltpu.get_barrier_semaphore()
     for device in (sibling, after_same, before_same, before_other):
@@ -261,8 +259,9 @@
     def _():
         pl.semaphore_signal(barrier, inc=1, device_id=below, device_id_type=MESH)
 
-    total[...] = jnp.zeros_like(total)
-    losses[...] = jnp.zeros_like(losses)
+    for copy in copies:
+        copy.wait()
+    held[slot(B_NEAR, z)] = unit(core)[0].astype(jnp.bfloat16)
     edges = jnp.where(z > 0, 1, 0) + jnp.where(z < deep - 1, 1, 0)
     pl.semaphore_wait(barrier, 4 + edges)
 
@@ -326,8 +325,8 @@
 
     def loss_copy():
         return pltpu.make_async_remote_copy(
-            src_ref=losses.at[2],
-            dst_ref=loss_in,
+            src_ref=loss_row.at[0],
+            dst_ref=loss_row.at[1],
             send_sem=sum_sem.at[2],
             recv_sem=sum_sem.at[3],
             device_id=outer,
@@ -385,6 +384,15 @@
 
     own_a, own_b = slot(A_NEAR, z), slot(B_NEAR, z)
 
+    def in_row(role):
+        return lax.dot_general(
+            jnp.ones((8, LANES), jnp.float32),
+            losses[role],
+            (((1,), (1,)), ((), ())),
+            precision=lax.Precision.HIGHEST,
+            preferred_element_type=jnp.float32,
+        )
+
     def near(zp):
         first = jnp.where(short(zp), 0, jnp.where(beyond(zp), 1, 0))
 
@@ -466,6 +474,7 @@
 
                 @pl.when(z == 1)
                 def _():
+                    loss_row[0] = in_row(2)
                     loss_copy().start()
 
             return carry
@@ -486,9 +495,21 @@
             action(behind)
 
     def turn(distance, carry):
-        for step in (pass_b, pass_a):
-            for part in range(PARTS):
-                both_ways(distance, functools.partial(step, distance=distance, part=part))
+        for part in range(PARTS):
+            both_ways(distance, functools.partial(pass_b, distance=distance, part=part))
+
+        @pl.when(distance == 0)
+        def _():
+            held[slot(A_NEAR, z)] = unit(1 - core)[0].astype(jnp.bfloat16)
+
+        for part in range(PARTS):
+            both_ways(distance, functools.partial(pass_a, distance=distance, part=part))
+
+        @pl.when(distance == 0)
+        def _():
+            total[...] = jnp.zeros_like(total)
+            losses[...] = jnp.zeros_like(losses)
+
         both_ways(distance, near)
         pl.when((distance == 0) & at_end)(relay)
         both_ways(distance - 1, far)
@@ -502,20 +523,20 @@
         role = jnp.where(a_end, 1, 0)
         total[role] += sums[1].astype(jnp.float32)
 
-        @pl.when(z == 0)
-        def _():
-            loss_copy().wait_recv()
-            losses[role] += loss_in[...]
-
-    def finish(ref, role):
-        unit32, inverse = unit(ref)
+    def finish(which, role):
+        unit32, inverse = unit(which)
         grad = total[role]
         along = jnp.sum(unit32 * grad, axis=-1, keepdims=True)
         return inverse * (grad - unit32 * along)
 
-    grad_img_ref[...] = finish(img_ref, core)
-    grad_txt_ref[...] = finish(txt_ref, 1 - core)
-    loss_ref[...] = jnp.sum(losses[core], axis=-1, keepdims=True)
+    grad_img_ref[...] = finish(0, core)
+    grad_txt_ref[...] = finish(1, 1 - core)
+    loss_ref[...] = in_row(core)[0:1]
+
+    @pl.when(z == 0)
+    def _():
+        loss_copy().wait_recv()
+        loss_ref[...] += loss_row[1, 0:1]
 
     def settle(zp, carry):
         for went, send in (
@@ -547,19 +568,21 @@
     loss, grad_images, grad_texts = pl.pallas_call(
         functools.partial(column_kernel, columns, deep),
         out_shape=(
-            jax.ShapeDtypeStruct((rows, 1), jnp.float32),
+            jax.ShapeDtypeStruct((1, rows), jnp.float32),
             jax.ShapeDtypeStruct((rows, width), jnp.float32),
             jax.ShapeDtypeStruct((rows, width), jnp.float32),
         ),
         in_specs=[pl.BlockSpec(memory_space=pltpu.SMEM)] * 2
-        + [pl.BlockSpec(memory_space=pltpu.VMEM)] * 2,
+        + [pl.BlockSpec(memory_space=pl.ANY)] * 2,
         out_specs=[pl.BlockSpec(memory_space=pltpu.VMEM)] * 3,
         scratch_shapes=[
             pltpu.VMEM((KINDS * deep, rows, width), jnp.bfloat16),
             pltpu.VMEM((3, rows, width), jnp.float32),
             pltpu.VMEM((3, rows, LANES), jnp.float32),
             pltpu.VMEM((2, rows, width), jnp.bfloat16),
-            pltpu.VMEM((rows, LANES), jnp.float32),
+            pltpu.VMEM((2, 8, rows), jnp.float32),
+            pltpu.VMEM((2, rows, width), jnp.bfloat16),
+            pltpu.SemaphoreType.DMA((2,)),
             pltpu.SemaphoreType.DMA((SENDS * deep, PARTS)),
             pltpu.SemaphoreType.DMA((KINDS * deep, PARTS)),
             pltpu.SemaphoreType.DMA((4,)),

time: 93.7 us -> 90.8 us (0.969)
  Pallas kernels: 86.4 us -> 83.6 us
    pallas_call x1, Pallas kernels: 86.4 us -> 83.6 us  [on_column(): pl.pallas_call(functools.partial(column_kernel, columns, deep), out_shape...]
    unnamed x6 -> x7, local copies, waits for them, and re-layouts: 4.15 us -> 4.71 us
where the time goes in v3:
time: 90.8 us; the launch traced here: 90.2 us
  Pallas kernels  83.6 us (92%)
  local copies, waits for them, and re-layouts  4.71 us (5%)
  between operations  1.94 us (2%)
    pallas_call x1, Pallas kernels, on_column(): pl.pallas_call(functools.partial(column_kernel, columns, deep), out_shape...  83.6 us
    unnamed x7, local copies, waits for them, and re-layouts  4.71 us

profile of v3, /device:TPU:1, one launch (start us, length us, event | category | flops | bytes accessed | tf_op | source)
XLA Modules:
  0.0 90.2 jit_solution(11370085871054504842)
XLA Ops:
  1.9 0.0 copy-start
  1.9 1.1 %copy-done = bf16[256,1152]{1,0:T(8,128)(2,1)S(1)} copy-done((bf16[256,1152]{1,0:T(8,128)(2,1)S(1)}, bf16[256,1152]{1,0:T(8,128)(2,1)}, u32[]{:S(2)}) %copy-start) | copy-done | bytes 589848
  3.0 0.0 copy-start.1
  3.0 1.1 %copy-done.1 = bf16[256,1152]{1,0:T(8,128)(2,1)S(1)} copy-done((bf16[256,1152]{1,0:T(8,128)(2,1)S(1)}, bf16[256,1152]{1,0:T(8,128)(2,1)}, u32[]{:S(2)}) %copy-start.1) | copy-done | bytes 589848
  4.1 83.6 %column.1 = (f32[1,256]{1,0:T(1,128)S(1)}, f32[256,1152]{1,0:T(8,128)S(1)}, f32[256,1152]{1,0:T(8,128)S(1)}) custom-call(f32[1]{0:T(128)S(6)} %copy.10.scale_ref, f32[1]{0:T(128)S(6)} %copy.11.offset_ref, bf16[256,1152]{1,0:T(8,128)(2,1)S(1)} %copy-done, bf16[256,1152]{1,0:T(8,128)(2,1)S(1)} %copy-done.1), custom_call_target="tpu_custom_call" | custom-call | flops 4831838208 | bytes 3538944 | tf_op jit(solution)/shard_map/column/pallas_call | solution.py:568
  87.6 0.6 copy.12
  88.2 1.0 %copy.13 = f32[256,1152]{1,0:T(8,128)} copy(f32[256,1152]{1,0:T(8,128)S(1)} %get-tuple-element.13) | data formatting | bytes 2359296
  89.2 1.0 %copy.14 = f32[256,1152]{1,0:T(8,128)} copy(f32[256,1152]{1,0:T(8,128)S(1)} %get-tuple-element.14) | data formatting | bytes 2359296
Async XLA Ops:
  1.9 1.1 %copy-start = (bf16[256,1152]{1,0:T(8,128)(2,1)S(1)}, bf16[256,1152]{1,0:T(8,128)(2,1)}, u32[]{:S(2)}) copy-start(bf16[256,1152]{1,0:T(8,128)(2,1)} %img_hbm.1) | copy-start | bytes 1769476
  3.0 1.1 %copy-start.1 = (bf16[256,1152]{1,0:T(8,128)(2,1)S(1)}, bf16[256,1152]{1,0:T(8,128)(2,1)}, u32[]{:S(2)}) copy-start(bf16[256,1152]{1,0:T(8,128)(2,1)} %txt_hbm.1) | copy-start | bytes 1769476

commit v4 on v3

--- a/solution.py
+++ b/solution.py
@@ -115,7 +115,7 @@
 SENDS = 10
 LANES = 128
 LOG2E = 1.4426950408889634
-PARTS = 2
+PARTS = 4
 
 
 def column_kernel(
@@ -517,20 +517,29 @@
 
     lax.fori_loop(0, deep + 1, turn, 0)
 
+    def finish(which, role, ref):
+        unit32, inverse = unit(which)
+        grad = total[role]
+        along = jnp.sum(unit32 * grad, axis=-1, keepdims=True)
+        ref[...] = inverse * (grad - unit32 * along)
+
+    def finish_images():
+        finish(0, core, grad_img_ref)
+
+    def finish_texts():
+        finish(1, 1 - core, grad_txt_ref)
+
+    pl.when(z == 0)(finish_texts)
+    pl.when(z != 0)(finish_images)
+
     @pl.when(at_end)
     def _():
         sum_copy().wait_recv()
         role = jnp.where(a_end, 1, 0)
         total[role] += sums[1].astype(jnp.float32)
 
-    def finish(which, role):
-        unit32, inverse = unit(which)
-        grad = total[role]
-        along = jnp.sum(unit32 * grad, axis=-1, keepdims=True)
-        return inverse * (grad - unit32 * along)
-
-    grad_img_ref[...] = finish(0, core)
-    grad_txt_ref[...] = finish(1, 1 - core)
+    pl.when(z == 0)(finish_images)
+    pl.when(z != 0)(finish_texts)
     loss_ref[...] = in_row(core)[0:1]
 
     @pl.when(z == 0)

time: 90.8 us -> 91.9 us (1.012)
    pallas_call x1, Pallas kernels: 83.6 us -> 84.5 us  [on_column(): pl.pallas_call(functools.partial(column_kernel, columns, deep), out_shape...]
where the time goes in v4:
time: 91.9 us; the launch traced here: 91.2 us
  Pallas kernels  84.5 us (92%)
  local copies, waits for them, and re-layouts  4.71 us (5%)
  between operations  1.94 us (2%)
    pallas_call x1, Pallas kernels, on_column(): pl.pallas_call(functools.partial(column_kernel, columns, deep), out_shape...  84.5 us
    unnamed x7, local copies, waits for them, and re-layouts  4.71 us

profile of v4, /device:TPU:1, one launch (start us, length us, event | category | flops | bytes accessed | tf_op | source)
XLA Modules:
  0.0 91.2 jit_solution(883191917537916573)
XLA Ops:
  1.9 0.0 copy-start
  1.9 1.1 %copy-done = bf16[256,1152]{1,0:T(8,128)(2,1)S(1)} copy-done((bf16[256,1152]{1,0:T(8,128)(2,1)S(1)}, bf16[256,1152]{1,0:T(8,128)(2,1)}, u32[]{:S(2)}) %copy-start) | copy-done | bytes 589848
  3.0 0.0 copy-start.1
  3.0 1.1 %copy-done.1 = bf16[256,1152]{1,0:T(8,128)(2,1)S(1)} copy-done((bf16[256,1152]{1,0:T(8,128)(2,1)S(1)}, bf16[256,1152]{1,0:T(8,128)(2,1)}, u32[]{:S(2)}) %copy-start.1) | copy-done | bytes 589848
  4.1 84.5 %column.1 = (f32[1,256]{1,0:T(1,128)S(1)}, f32[256,1152]{1,0:T(8,128)S(1)}, f32[256,1152]{1,0:T(8,128)S(1)}) custom-call(f32[1]{0:T(128)S(6)} %copy.10.scale_ref, f32[1]{0:T(128)S(6)} %copy.11.offset_ref, bf16[256,1152]{1,0:T(8,128)(2,1)S(1)} %copy-done, bf16[256,1152]{1,0:T(8,128)(2,1)S(1)} %copy-done.1), custom_call_target="tpu_custom_call" | custom-call | flops 4831838208 | bytes 3538944 | tf_op jit(solution)/shard_map/column/pallas_call | solution.py:577
  88.6 0.6 copy.12
  89.1 1.0 %copy.13 = f32[256,1152]{1,0:T(8,128)} copy(f32[256,1152]{1,0:T(8,128)S(1)} %get-tuple-element.13) | data formatting | bytes 2359296
  90.2 1.0 %copy.14 = f32[256,1152]{1,0:T(8,128)} copy(f32[256,1152]{1,0:T(8,128)S(1)} %get-tuple-element.14) | data formatting | bytes 2359296
Async XLA Ops:
  1.9 1.1 %copy-start = (bf16[256,1152]{1,0:T(8,128)(2,1)S(1)}, bf16[256,1152]{1,0:T(8,128)(2,1)}, u32[]{:S(2)}) copy-start(bf16[256,1152]{1,0:T(8,128)(2,1)} %img_hbm.1) | copy-start | bytes 1769476
  3.0 1.1 %copy-start.1 = (bf16[256,1152]{1,0:T(8,128)(2,1)S(1)}, bf16[256,1152]{1,0:T(8,128)(2,1)}, u32[]{:S(2)}) copy-start(bf16[256,1152]{1,0:T(8,128)(2,1)} %txt_hbm.1) | copy-start | bytes 1769476

commit v5 on v4

--- a/solution.py
+++ b/solution.py
@@ -115,7 +115,7 @@
 SENDS = 10
 LANES = 128
 LOG2E = 1.4426950408889634
-PARTS = 4
+PARTS = 2
 
 
 def column_kernel(
@@ -597,7 +597,7 @@
             pltpu.SemaphoreType.DMA((4,)),
         ],
         compiler_params=pltpu.CompilerParams(
-            collective_id=0, has_side_effects=True, vmem_limit_bytes=48 * 1024 * 1024
+            collective_id=0, has_side_effects=True, vmem_limit_bytes=60 * 1024 * 1024
         ),
         cost_estimate=pl.CostEstimate(
             flops=tiles * 4 * rows * rows * width,

time: 91.9 us -> 91.8 us (level)
    unnamed x7 -> x5, local copies, waits for them, and re-layouts: 4.71 us -> 4.71 us
where the time goes in v5:
time: 91.8 us; the launch traced here: 91.2 us
  Pallas kernels  84.6 us (92%)
  local copies, waits for them, and re-layouts  4.71 us (5%)
  between operations  1.93 us (2%)
    pallas_call x1, Pallas kernels, on_column(): pl.pallas_call(functools.partial(column_kernel, columns, deep), out_shape...  84.6 us
    unnamed x5, local copies, waits for them, and re-layouts  4.71 us

profile of v5, /device:TPU:1, one launch (start us, length us, event | category | flops | bytes accessed | tf_op | source)
XLA Modules:
  0.0 91.2 jit_solution(3219932924196795644)
XLA Ops:
  1.9 84.6 %column.1 = (f32[1,256]{1,0:T(1,128)}, f32[256,1152]{1,0:T(8,128)}, f32[256,1152]{1,0:T(8,128)}) custom-call(f32[1]{0:T(128)S(6)} %copy.10.scale_ref, f32[1]{0:T(128)S(6)} %copy.11.offset_ref, bf16[256,1152]{1,0:T(8,128)(2,1)} %img_hbm.1, bf16[256,1152]{1,0:T(8,128)(2,1)} %txt_hbm.1), custom_call_target="tpu_custom_call" | custom-call | flops 4831838208 | bytes 3538944 | tf_op jit(solution)/shard_map/column/pallas_call | solution.py:577
  86.5 1.2 %copy.12 = f32[256]{0:T(256)} copy(f32[256]{0:T(256)} %bitcast.1) | data formatting | bytes 2048
  87.8 0.0 copy-start
  87.8 2.5 %copy.13 = f32[256,1152]{1,0:T(8,128)} copy(f32[256,1152]{1,0:T(8,128)} %get-tuple-element.13) | data formatting | bytes 2359296
  90.2 0.0 copy-done
  90.2 1.0 %copy.14 = f32[256,1152]{1,0:T(8,128)} copy(f32[256,1152]{1,0:T(8,128)S(1)} %copy-done) | data formatting | bytes 2359296
Async XLA Ops:
  87.8 2.5 %copy-start = (f32[256,1152]{1,0:T(8,128)S(1)}, f32[256,1152]{1,0:T(8,128)}, u32[]{:S(2)}) copy-start(f32[256,1152]{1,0:T(8,128)} %get-tuple-element.14) | copy-start | bytes 3538948
